TPU v7x, 32 devices: a whole 2x2x4 slice. The times are simulated.
32 devices in a mesh: parts: 1, ctx: 32 (over z, y, x, core).
Axes of the slice: x: 2, y: 2, z: 4, core: 2. Of those that a mesh axis runs over, the one named last changes fastest.
Arguments:
- hidden_states: bfloat16 [2048, 2880], P(('parts', 'ctx')), may hold values from -6 to 6
- o_proj: bfloat16 [2048, 2880], P('ctx'), may hold values from -1 to 1
- norm_gain: bfloat16 [2880], replicated, may hold values from 0.099609375 to 1.8984375
- router_weight: bfloat16 [2880, 8], replicated, may hold values from -0.109375 to 0.109375
- routes: int32 [2048, 4], P(('parts', 'ctx')), may hold values from 0 to 7, all different within a row; in each aligned block of 64 rows (0 to 63, 64 to 127, ...) at most 36 rows name the same one
- w_gate: bfloat16 [32, 2880, 360], P('ctx'), may hold values from -0.109375 to 0.109375
- w_up: bfloat16 [32, 2880, 360], P('ctx'), may hold values from -0.109375 to 0.109375
- w_down: bfloat16 [32, 360, 2880], P('ctx'), may hold values from -0.15625 to 0.15625
- query: bfloat16 [2048, 2048], P(('parts', 'ctx')), may hold values from -6 to 6
- keys: bfloat16 [2048, 256], P(('parts', 'ctx')), may hold values from -6 to 6
- values: bfloat16 [2048, 256], P(('parts', 'ctx')), may hold values from -6 to 6
Outputs:
- moe_output: bfloat16 [2048, 2880], P(('parts', 'ctx'))
- attended: bfloat16 [2048, 2048], P(('parts', 'ctx'))
Inputs may be any that keep to these rules, and one draw needn't show every extreme that they name: `routes`: each row names 4 different experts; the rows of one device name no expert more than 36 times, and in every draw some device names some expert exactly 36 times.
All inputs are finite; a program needn't handle non-finite values.
Results may differ from a plain program's by a relative error of at most 0.012.
Values may be sent and summed in bfloat16 or wider, within the bound.
A program may use at most 128 MiB of HBM per device.

v0:
```python
import jax
import jax.numpy as jnp
from jax import lax
from jax.sharding import PartitionSpec as P

HEADS = 32
KV_HEADS = 4
HEAD_DIM = 64


def from_behind(block, axis, distance):
    devices = range(lax.axis_size(axis))
    route = [(i - distance, i) for i in devices if i - distance in devices]
    return lax.ppermute(block, axis, route)


def attend_block(query_rows, key_rows, value_rows, span, tok_rows):
    group_size = HEADS // KV_HEADS
    queries = query_rows.reshape(tok_rows, KV_HEADS, group_size, HEAD_DIM)
    key_grid = key_rows.reshape(4 * tok_rows, KV_HEADS, HEAD_DIM)
    value_grid = value_rows.reshape(4 * tok_rows, KV_HEADS, HEAD_DIM)
    scores = jnp.einsum(
        "tgrd,pgd->grtp", queries, key_grid, preferred_element_type=jnp.float32
    ) * HEAD_DIM ** (-0.5)
    query_pos = span * tok_rows + jnp.arange(tok_rows, dtype=jnp.int32)
    key_pos = (span - 3) * tok_rows + jnp.arange(4 * tok_rows, dtype=jnp.int32)
    allowed = (key_pos[None, :] >= 0) & (key_pos[None, :] <= query_pos[:, None])
    scores = jnp.where(allowed, scores, -1e30)
    top_score = jnp.max(scores, axis=-1, keepdims=True)
    weights = jnp.where(allowed, jnp.exp(scores - top_score), 0.0)
    probs = (weights / jnp.sum(weights, axis=-1, keepdims=True)).astype(jnp.bfloat16)
    mixed_heads = jnp.einsum(
        "grtp,pgd->tgrd", probs, value_grid, preferred_element_type=jnp.float32
    )
    return mixed_heads.reshape(tok_rows, HEADS * HEAD_DIM).astype(jnp.bfloat16)


def local(
    hidden_states,
    o_proj,
    norm_gain,
    router_weight,
    routes,
    w_gate,
    w_up,
    w_down,
    query,
    keys,
    values,
):
    tok_rows = hidden_states.shape[0]
    model_width = hidden_states.shape[1]
    per_token = routes.shape[1]
    experts = router_weight.shape[1]
    devices = lax.axis_size("ctx")
    shard_count = devices // experts
    capacity = min(tok_rows, (tok_rows * per_token // experts // shard_count + 1) * shard_count)
    span = lax.axis_index("ctx")
    kv_pair = jnp.stack([keys, values])
    pieces = [kv_pair]
    current = kv_pair
    for step_index in range(3):
        current = from_behind(current, "ctx", 1)
        pieces.append(current)
    window = jnp.concatenate(pieces[::-1], axis=1)
    attended = attend_block(query, window[0], window[1], span, tok_rows)
    projected = jnp.dot(
        attended,
        lax.all_gather(o_proj, "ctx", axis=0, tiled=True),
        preferred_element_type=jnp.float32,
    )
    stream = (hidden_states.astype(jnp.float32) + projected).astype(jnp.bfloat16)
    features = stream.astype(jnp.float32)
    normed = (
        features
        * lax.rsqrt(jnp.mean(features * features, axis=-1, keepdims=True) + 1e-05)
        * norm_gain.astype(jnp.float32)
    ).astype(jnp.bfloat16)
    logits = jnp.dot(normed, router_weight, preferred_element_type=jnp.float32)
    picked = jnp.take_along_axis(logits, routes, axis=1)
    route_weight = jax.nn.softmax(picked, axis=-1)
    flat_expert = routes.reshape(-1)
    flat_token = jnp.arange(tok_rows * per_token, dtype=jnp.int32) // per_token
    onehot = (flat_expert[:, None] == jnp.arange(experts, dtype=jnp.int32)[None, :]).astype(
        jnp.int32
    )
    slot_rank = jnp.sum((jnp.cumsum(onehot, axis=0) - 1) * onehot, axis=1)
    buffer = (
        jnp.zeros((experts, capacity, model_width), jnp.bfloat16)
        .at[flat_expert, slot_rank]
        .set(normed[flat_token])
    )
    outgoing = jnp.broadcast_to(buffer[:, None], (experts, shard_count, capacity, model_width))
    outgoing = outgoing.reshape(devices, capacity, model_width)
    received = lax.all_to_all(outgoing, "ctx", split_axis=0, concat_axis=0, tiled=True)
    slot_count = received.shape[1]
    rows_flat = received.reshape(devices * slot_count, model_width)
    gate_val = jnp.dot(rows_flat, w_gate[0], preferred_element_type=jnp.float32)
    up_val = jnp.dot(rows_flat, w_up[0], preferred_element_type=jnp.float32)
    activated = ((up_val + 1.0) * gate_val * jax.nn.sigmoid(1.702 * gate_val)).astype(jnp.bfloat16)
    piece = jnp.dot(activated, w_down[0], preferred_element_type=jnp.float32).astype(jnp.bfloat16)
    returned = lax.all_to_all(
        piece.reshape(devices, slot_count, model_width),
        "ctx",
        split_axis=0,
        concat_axis=0,
        tiled=True,
    )
    shard_total = (
        returned.reshape(experts, shard_count, capacity, model_width)
        .astype(jnp.float32)
        .sum(axis=1)
    )
    summed = lax.optimization_barrier(shard_total.astype(jnp.bfloat16)).astype(jnp.float32)
    per_choice = summed[flat_expert, slot_rank] * route_weight.reshape(-1)[:, None]
    moe_output = (
        features + per_choice.reshape(tok_rows, per_token, model_width).sum(axis=1)
    ).astype(jnp.bfloat16)
    return (moe_output, attended)


def solution(mesh):
    in_specs = (
        P(("parts", "ctx"), None),
        P("ctx", None),
        P(),
        P(),
        P(("parts", "ctx"), None),
        P("ctx", None, None),
        P("ctx", None, None),
        P("ctx", None, None),
        P(("parts", "ctx"), None),
        P(("parts", "ctx"), None),
        P(("parts", "ctx"), None),
    )
    out_specs = (P(("parts", "ctx"), None), P(("parts", "ctx"), None))
    return jax.shard_map(local, mesh=mesh, in_specs=in_specs, out_specs=out_specs, check_vma=False)
```

profile of v0, /device:TPU:10, one launch (start us, length us, event | category | flops | bytes accessed | tf_op | source)
XLA Modules:
  0.0 581.4 jit_solution(6661537492269090085)
XLA Ops:
  7.9 0.8 pad_maximum_fusion
  8.7 1.9 collective-permute-start
  13.5 1.5 reshape.190
  15.0 3.5 collective-permute-start.1
  18.5 2.1 collective-permute-done.1
  20.6 1.9 collective-permute-start.2
  22.5 3.6 collective-permute-done.2
  26.1 0.8 maximum_maximum_fusion
  27.2 2.3 fusion.32
  29.5 3.2 convolution_convert_fusion.1
  32.6 72.6 %all-gather.2.cloned.1.call-done = bf16[2048,2880]{1,0:T(8,128)(2,1)} async-done(((bf16[64,2880]{1,0:T(8,128)(2,1)}), bf16[2048,2880]{1,0:T(8,128)(2,1)}) %all-gather.2.cloned.1.call-update) | async-done | bytes 11796496 | tf_op jit(solution)/shard_map/all_gather | solution.py:69
  105.3 6.7 %multiply_reduce_fusion.1 = (f32[64]{0:T(128)S(1)}, f32[64,2880]{1,0:T(8,128)S(1)}) fusion(bf16[64,2048]{0,1:T(8,128)(2,1)} %bitcast.61, bf16[2048,2880]{1,0:T(8,128)(2,1)} %all-gather.2.cloned.1.call-done, bf16[64,2880]{1,0:T(8,128)(2,1)S(1)} %copy-done.6), kind=kOutput, calls=%fused_computation.30 | convolution fusion | flops 756080576 | bytes 13164800 | tf_op jit(solution)/shard_map/dot_general | solution.py:67
  112.2 2.7 gather_fusion
  114.8 1.3 broadcast_in_dim.23
  116.1 57.4 %scatter_fusion = bf16[8,36,2880]{2,0,1:T(8,128)(2,1)} fusion(bf16[8,36,2880]{2,0,1:T(8,128)(2,1)} %broadcast_in_dim.23, s32[256]{0:T(256)S(1)} %bitcast.59, bf16[256,2880]{1,0:T(8,128)(2,1)} %gather_fusion), kind=kCustom, calls=%fused_computation.3 | custom fusion | bytes 4425728 | tf_op jit(solution)/shard_map/scatter | solution.py:91
  173.5 1.6 copy.54
  175.7 167.8 %all_to_all.10 = bf16[32,36,2880]{2,1,0:T(8,128)(2,1)} all-to-all(bf16[32,36,2880]{2,1,0:T(8,128)(2,1)S(1)} %bitcast.58), channel_id=1, replica_groups=mesh['parts'=1,'ctx'=32] {'ctx'}, dimensions={0} | all-to-all | bytes 13271040 | tf_op jit(solution)/shard_map/all_to_all | solution.py:95
  343.4 9.3 %reshape.194 = bf16[1152,2880]{1,0:T(8,128)(2,1)} reshape(bf16[32,36,2880]{2,1,0:T(8,128)(2,1)} %all_to_all.10) | data formatting | bytes 13271040 | tf_op jit(solution)/shard_map/reshape | solution.py:97
  352.7 6.7 %fusion.7 = f32[1152,360]{0,1:T(8,128)S(1)} fusion(bf16[1152,2880]{1,0:T(8,128)(2,1)} %reshape.194, bf16[1,2880,360]{1,2,0:T(8,128)(2,1)} %param.16), kind=kOutput, calls=%fused_computation.16 | convolution fusion | flops 2388787200 | bytes 10368000 | tf_op jit(solution)/shard_map/dot_general | solution.py:98
  359.5 3.3 fusion.5
  362.8 6.0 %convolution_convert_fusion = bf16[1152,2880]{0,1:T(8,128)(2,1)} fusion(bf16[1152,360]{0,1:T(8,128)(2,1)S(1)} %fusion.5, bf16[1,360,2880]{2,1,0:T(8,128)(2,1)S(1)} %copy-done), kind=kOutput, calls=%fused_computation.5 | convolution fusion | flops 2392104960 | bytes 9538560 | tf_op jit(solution)/shard_map/dot_general | solution.py:101
  368.8 10.1 %copy.55 = bf16[1152,2880]{1,0:T(8,128)(2,1)} copy(bf16[1152,2880]{0,1:T(8,128)(2,1)} %convolution_convert_fusion) | data formatting | bytes 13271040 | tf_op jit(solution)/shard_map/convert_element_type | solution.py:101
  378.9 8.7 %reshape.195 = bf16[32,36,2880]{2,1,0:T(8,128)(2,1)} reshape(bf16[1152,2880]{1,0:T(8,128)(2,1)} %copy.55) | data formatting | bytes 13271040 | tf_op jit(solution)/shard_map/reshape | solution.py:103
  387.6 5.9 %all-to-all-start.1 = ((bf16[32,36,2880]{2,1,0:T(8,128)(2,1)}), bf16[32,36,2880]{2,1,0:T(8,128)(2,1)}, u32[]{:S(2)}, u32[]{:S(2)}) async-start(bf16[32,36,2880]{2,1,0:T(8,128)(2,1)} %reshape.195), calls=%async_computation.1 | async-start | bytes 15073280 | tf_op jit(solution)/shard_map/all_to_all | solution.py:102
  393.7 0.9 copy.60
  394.8 1.5 gather_fusion.2
  396.6 159.1 %all-to-all-done.1 = bf16[32,36,2880]{2,1,0:T(8,128)(2,1)} async-done(((bf16[32,36,2880]{2,1,0:T(8,128)(2,1)}), bf16[32,36,2880]{2,1,0:T(8,128)(2,1)}, u32[]{:S(2)}, u32[]{:S(2)}) %all-to-all-start.1) | async-done | bytes 6635552 | tf_op jit(solution)/shard_map/all_to_all | solution.py:102
  555.8 4.3 bitcast_reduce_fusion
  560.3 4.8 gather_fusion.1
  565.1 4.6 gather.14
  569.7 4.0 multiply_reduce_fusion
  573.7 0.8 add_convert_fusion
  (58 shorter events, 5.4 us)
Async XLA Ops:
  7.2 355.6 %copy-start = (bf16[1,360,2880]{2,1,0:T(8,128)(2,1)S(1)}, bf16[1,360,2880]{2,1,0:T(8,128)(2,1)}, u32[]{:S(2)}) copy-start(bf16[1,360,2880]{2,1,0:T(8,128)(2,1)} %param.18) | copy-start | bytes 6220804
  7.2 98.1 %all-gather.2.cloned.1.call-start = ((), (), s32[]{:S(2)}) async-start(), calls=%async_computation.2 | async-start | bytes 12435456 | tf_op jit(solution)/shard_map/all_gather | solution.py:69
  8.7 6.3 %collective-permute-start = (bf16[2,64,256]{2,1,0:T(8,128)(2,1)S(1)}, bf16[2,64,256]{2,1,0:T(8,128)(2,1)S(1)}, u32[]{:S(2)}, u32[]{:S(2)}) collective-permute-start(bf16[2,64,256]{2,1,0:T(8,128)(2,1)S(1)} %pad_maximum_fusion), channel_id=1, source_target_pairs={{0,1},{1,2},{2,3},{3,4},{4,5},{5,6},{6,7},{7,8},{8,9},{9,10},{10,1... | collective-permute-start | bytes 196616 | tf_op jit(solution)/shard_map/ppermute | solution.py:14
  15.0 5.6 collective-permute-start.1
  20.6 5.6 collective-permute-start.2
  29.5 75.8 %copy-start.6 = (bf16[64,2880]{1,0:T(8,128)(2,1)S(1)}, bf16[64,2880]{1,0:T(8,128)(2,1)}, u32[]{:S(2)}) copy-start(bf16[64,2880]{1,0:T(8,128)(2,1)} %param.11) | copy-start | bytes 1105924
  112.0 2.8 copy-start.2
  352.7 6.7 %copy-start.4 = (bf16[1152,2880]{1,0:T(8,128)(2,1)S(1)}, bf16[1152,2880]{1,0:T(8,128)(2,1)}, u32[]{:S(2)}) copy-start(bf16[1152,2880]{1,0:T(8,128)(2,1)} %reshape.194) | copy-start | bytes 19906564
  352.7 6.7 %copy-start.9 = (bf16[1,2880,360]{1,2,0:T(8,128)(2,1)S(1)}, bf16[1,2880,360]{1,2,0:T(8,128)(2,1)}, u32[]{:S(2)}) copy-start(bf16[1,2880,360]{1,2,0:T(8,128)(2,1)} %param.17) | copy-start | bytes 6220804
  387.6 5.9 %copy-start.8 = (s32[64,4]{0,1:T(4,128)S(1)}, s32[64,4]{0,1:T(4,128)}, u32[]{:S(2)}) copy-start(s32[64,4]{0,1:T(4,128)} %param.15) | copy-start | bytes 3076
  387.6 6.1 %copy-start.5 = (bf16[4,64,8,64]{3,1,2,0:T(8,128)(2,1)S(1)}, bf16[4,64,8,64]{3,1,2,0:T(8,128)(2,1)}, u32[]{:S(2)}) copy-start(bf16[4,64,8,64]{3,1,2,0:T(8,128)(2,1)} %convolution_convert_fusion.1) | copy-start | bytes 786436
  387.6 7.1 %copy-start.7 = (bf16[2880,8]{0,1:T(8,128)(2,1)S(1)}, bf16[2880,8]{0,1:T(8,128)(2,1)}, u32[]{:S(2)}) copy-start(bf16[2880,8]{0,1:T(8,128)(2,1)} %param.14) | copy-start | bytes 138244
  387.6 168.2 %all-to-all-start.1 = ((bf16[32,36,2880]{2,1,0:T(8,128)(2,1)}), bf16[32,36,2880]{2,1,0:T(8,128)(2,1)}, u32[]{:S(2)}, u32[]{:S(2)}) async-start(bf16[32,36,2880]{2,1,0:T(8,128)(2,1)} %reshape.195), calls=%async_computation.1 | async-start | bytes 15073280 | tf_op jit(solution)/shard_map/all_to_all | solution.py:102
  565.1 9.5 %copy-start.1 = (bf16[1,360,2880]{2,1,0:T(8,128)(2,1)S(1)}, bf16[1,360,2880]{2,1,0:T(8,128)(2,1)}, u32[]{:S(2)}) copy-start(bf16[1,360,2880]{2,1,0:T(8,128)(2,1)} %param.18) | copy-start | bytes 6220804
  569.7 4.0 copy-start.3
Sparse Core Ops, SparseCore 0:
  10.8 94.3 all-gather.1
where the time goes:
time: 590 us; the launch traced here: 581 us
  waiting for transfers between devices  238 us (40%)
  blocking collectives  168 us (28%)
  local copies, waits for them, and re-layouts  107 us (18%)
  matrix products  28.4 us (5%)
  between operations  14.3 us (2%)
  starting transfers between devices  13.3 us (2%)
  other arithmetic  12.7 us (2%)
    all_to_all x1, blocking collectives, local(): lax.all_to_all(outgoing, 'ctx', split_axis=0, concat_axis=0, tiled=True)  168 us
    all_to_all x1, waiting for transfers between devices, local(): lax.all_to_all(piece.reshape(devices, slot_count, model_width), 'ctx', sp...  159 us
    all_gather x1, waiting for transfers between devices, local(): lax.all_gather(o_proj, 'ctx', axis=0, tiled=True)  72.6 us
    scatter x2, local copies, waits for them, and re-layouts, local(): buffer = jnp.zeros((experts, capacity, model_width), jnp.bfloat16).at[fla...  59 us
  transfers between devices with their start and end apart: 5, of which 4 were waited for; matrix products, arithmetic and copies ran while one was open for 3% of the time, Pallas kernels for 0%

commit v1 on v0

--- a/solution.py
+++ b/solution.py
@@ -1,6 +1,10 @@
+import functools
+
 import jax
 import jax.numpy as jnp
 from jax import lax
+from jax.experimental import pallas as pl
+from jax.experimental.pallas import tpu as pltpu
 from jax.sharding import PartitionSpec as P
 
 HEADS = 32
@@ -33,6 +37,238 @@
         "grtp,pgd->tgrd", probs, value_grid, preferred_element_type=jnp.float32
     )
     return mixed_heads.reshape(tok_rows, HEADS * HEAD_DIM).astype(jnp.bfloat16)
+
+
+MEMBERS = 4
+
+
+def expert_kernel(
+    groups,
+    slab_ref,
+    gate_hbm,
+    up_hbm,
+    down_hbm,
+    out_ref,
+    recv,
+    pieces,
+    near,
+    pair_sum,
+    far,
+    final,
+    gate_ref,
+    up_ref,
+    down_ref,
+    weight_sem,
+    send_sem,
+    recv_sem,
+):
+    me = lax.axis_index("ctx")
+    group = me // MEMBERS
+    j = me % MEMBERS
+    j_sib = j + 1 - 2 * (j % 2)
+    j_far = (j + 2) % MEMBERS
+    j_diag = MEMBERS - 1 - j
+    sibling = group * MEMBERS + j_sib
+    partner = group * MEMBERS + j_far
+
+    def to(src, dst, kind, here, there, device):
+        return pltpu.make_async_remote_copy(
+            src_ref=src,
+            dst_ref=dst,
+            send_sem=send_sem.at[kind, here],
+            recv_sem=recv_sem.at[kind, there],
+            device_id={"ctx": device},
+            device_id_type=pl.DeviceIdType.MESH,
+        )
+
+    weight_copies = [
+        pltpu.make_async_copy(src, dst, weight_sem.at[i])
+        for i, (src, dst) in enumerate(
+            ((gate_hbm.at[0], gate_ref), (up_hbm.at[0], up_ref), (down_hbm.at[0], down_ref))
+        )
+    ]
+    for copy in weight_copies:
+        copy.start()
+
+    barrier = pltpu.get_barrier_semaphore()
+
+    def greet(device):
+        pl.semaphore_signal(
+            barrier, inc=1, device_id={"ctx": device}, device_id_type=pl.DeviceIdType.MESH
+        )
+
+    @pl.loop(1, groups)
+    def _(o):
+        greet(lax.rem(group + o, groups) * MEMBERS + j)
+
+    greet(sibling)
+    greet(partner)
+    pl.semaphore_wait(barrier, groups + 1)
+
+    def scatter(target):
+        return to(
+            slab_ref.at[target], recv.at[group, j], 0, target, group, target * MEMBERS + j
+        )
+
+    def scattered(s):
+        return to(slab_ref.at[s], recv.at[s, j], 0, s, s, sibling)
+
+    def share_sibling(s):
+        return to(recv.at[s, j], recv.at[s, j], 1, s, s, sibling)
+
+    def share_partner(s):
+        return to(recv.at[s, j], recv.at[s, j], 2, s, s, partner)
+
+    def share_diag(s):
+        return to(recv.at[s, j_far], recv.at[s, j_far], 3, s, s, sibling)
+
+    def piece_near(s):
+        return to(pieces.at[s, j_sib], near.at[s, 0], 4, s, s, sibling)
+
+    def piece_diag(s):
+        return to(pieces.at[s, j_diag], near.at[s, 1], 5, s, s, sibling)
+
+    def piece_far(s):
+        return to(pair_sum.at[s], far.at[s], 6, s, s, partner)
+
+    def give_back(s):
+        return to(final.at[s], out_ref.at[group], 7, s, group, s * MEMBERS + j)
+
+    def given_back(s):
+        return to(final.at[s], out_ref.at[s], 7, s, s, s * MEMBERS + j)
+
+    @pl.loop(1, groups)
+    def _(o):
+        scatter(lax.rem(group + o, groups)).start()
+
+    recv[group, j] = slab_ref[group]
+
+    def source(step):
+        return lax.rem(group - step + groups, groups)
+
+    rows, width = recv.shape[2], recv.shape[3]
+
+    @pl.loop(0, groups + 4)
+    def _(t):
+        @pl.when(t < groups)
+        def _():
+            s = source(t)
+
+            @pl.when(t > 0)
+            def _():
+                scattered(s).wait_recv()
+
+            share_partner(s).start()
+            share_sibling(s).start()
+
+        @pl.when((t >= 1) & (t < groups + 1))
+        def _():
+            s = source(t - 1)
+            share_partner(s).wait_recv()
+            share_diag(s).start()
+
+        @pl.when((t >= 4) & (t < groups + 4))
+        def _():
+            s = source(t - 4)
+            piece_far(s).wait_recv()
+            total = (
+                pieces[s, j].astype(jnp.float32)
+                + near[s, 0].astype(jnp.float32)
+                + far[s].astype(jnp.float32)
+            ).astype(jnp.bfloat16)
+
+            @pl.when(t == 4)
+            def _():
+                out_ref[group] = total
+
+            @pl.when(t > 4)
+            def _():
+                final[s] = total
+                give_back(s).start()
+
+        @pl.when((t >= 3) & (t < groups + 3))
+        def _():
+            s = source(t - 3)
+            piece_near(s).wait_recv()
+            piece_diag(s).wait_recv()
+            pair_sum[s] = (
+                pieces[s, j_far].astype(jnp.float32) + near[s, 1].astype(jnp.float32)
+            ).astype(jnp.bfloat16)
+            piece_far(s).start()
+
+        @pl.when((t >= 2) & (t < groups + 2))
+        def _():
+            s = source(t - 2)
+
+            @pl.when(t == 2)
+            def _():
+                for copy in weight_copies:
+                    copy.wait()
+
+            share_sibling(s).wait_recv()
+            share_diag(s).wait_recv()
+            block = recv[s].reshape(MEMBERS * rows, width)
+            gate = jnp.dot(block, gate_ref[...], preferred_element_type=jnp.float32)
+            up = jnp.dot(block, up_ref[...], preferred_element_type=jnp.float32)
+            activated = ((up + 1.0) * gate * jax.nn.sigmoid(1.702 * gate)).astype(jnp.bfloat16)
+            for at in range(0, width, 768):
+                span = slice(at, min(at + 768, width))
+                piece = jnp.dot(
+                    activated, down_ref[:, span], preferred_element_type=jnp.float32
+                ).astype(jnp.bfloat16)
+                pieces[s, :, :, span] = piece.reshape(MEMBERS, rows, span.stop - span.start)
+            piece_near(s).start()
+            piece_diag(s).start()
+
+    @pl.loop(0, groups)
+    def _(s):
+        share_sibling(s).wait_send()
+        share_partner(s).wait_send()
+        share_diag(s).wait_send()
+        piece_near(s).wait_send()
+        piece_diag(s).wait_send()
+        piece_far(s).wait_send()
+
+    @pl.loop(1, groups)
+    def _(o):
+        s = source(o)
+        scattered(s).wait_send()
+        given_back(s).wait_send()
+        given_back(s).wait_recv()
+
+
+def experts_call(slabs, w_gate, w_up, w_down):
+    groups, slots, width = slabs.shape
+    hidden = w_gate.shape[2]
+    anywhere = pl.BlockSpec(memory_space=pl.ANY)
+    vmem = pl.BlockSpec(memory_space=pltpu.VMEM)
+
+    def buffer(*shape):
+        return pltpu.VMEM(shape, jnp.bfloat16)
+
+    return pl.pallas_call(
+        functools.partial(expert_kernel, groups),
+        out_shape=jax.ShapeDtypeStruct(slabs.shape, jnp.bfloat16),
+        in_specs=[vmem, anywhere, anywhere, anywhere],
+        out_specs=vmem,
+        scratch_shapes=[
+            buffer(groups, MEMBERS, slots, width),
+            buffer(groups, MEMBERS, slots, width),
+            buffer(groups, 2, slots, width),
+            buffer(groups, slots, width),
+            buffer(groups, slots, width),
+            buffer(groups, slots, width),
+            buffer(width, hidden),
+            buffer(width, hidden),
+            buffer(hidden, width),
+            pltpu.SemaphoreType.DMA((3,)),
+            pltpu.SemaphoreType.DMA((8, groups)),
+            pltpu.SemaphoreType.DMA((8, groups)),
+        ],
+        compiler_params=pltpu.CompilerParams(
+            collective_id=0, has_side_effects=True, vmem_limit_bytes=56 * 1024 * 1024
+        ),
+    )(slabs, w_gate, w_up, w_down)
 
 
 def local(
@@ -55,6 +291,7 @@
     devices = lax.axis_size("ctx")
     shard_count = devices // experts
     capacity = min(tok_rows, (tok_rows * per_token // experts // shard_count + 1) * shard_count)
+    slots = -(-capacity // 8) * 8
     span = lax.axis_index("ctx")
     kv_pair = jnp.stack([keys, values])
     pieces = [kv_pair]
@@ -77,45 +314,28 @@
         * norm_gain.astype(jnp.float32)
     ).astype(jnp.bfloat16)
     logits = jnp.dot(normed, router_weight, preferred_element_type=jnp.float32)
-    picked = jnp.take_along_axis(logits, routes, axis=1)
-    route_weight = jax.nn.softmax(picked, axis=-1)
-    flat_expert = routes.reshape(-1)
-    flat_token = jnp.arange(tok_rows * per_token, dtype=jnp.int32) // per_token
-    onehot = (flat_expert[:, None] == jnp.arange(experts, dtype=jnp.int32)[None, :]).astype(
-        jnp.int32
+    choices = jnp.arange(experts, dtype=jnp.int32)
+    named = jnp.any(routes[:, :, None] == choices, axis=1)
+    top_logit = jnp.max(jnp.where(named, logits, -jnp.inf), axis=-1, keepdims=True)
+    raw = jnp.where(named, jnp.exp(jnp.where(named, logits - top_logit, 0.0)), 0.0)
+    route_weight = raw / jnp.sum(raw, axis=-1, keepdims=True)
+    tokens = jnp.arange(tok_rows, dtype=jnp.int32)
+    earlier = (tokens[None, :] < tokens[:, None]).astype(jnp.bfloat16)
+    rank = jnp.dot(earlier, named.astype(jnp.bfloat16), preferred_element_type=jnp.float32)
+    slot_index = jnp.arange(slots, dtype=jnp.int32)
+    assign = named[:, :, None] & (rank.astype(jnp.int32)[:, :, None] == slot_index)
+    place = assign.astype(jnp.bfloat16).reshape(tok_rows, experts * slots)
+    slabs = lax.dot_general(
+        place, normed, (((0,), (0,)), ((), ())), preferred_element_type=jnp.float32
+    ).astype(jnp.bfloat16).reshape(experts, slots, model_width)
+    summed = experts_call(slabs, w_gate, w_up, w_down).reshape(experts * slots, model_width)
+    weights = jnp.where(assign, route_weight[:, :, None], 0.0).reshape(tok_rows, experts * slots)
+    upper = weights.astype(jnp.bfloat16)
+    lower = (weights - upper.astype(jnp.float32)).astype(jnp.bfloat16)
+    both = jnp.dot(
+        jnp.concatenate([upper, lower]), summed, preferred_element_type=jnp.float32
     )
-    slot_rank = jnp.sum((jnp.cumsum(onehot, axis=0) - 1) * onehot, axis=1)
-    buffer = (
-        jnp.zeros((experts, capacity, model_width), jnp.bfloat16)
-        .at[flat_expert, slot_rank]
-        .set(normed[flat_token])
-    )
-    outgoing = jnp.broadcast_to(buffer[:, None], (experts, shard_count, capacity, model_width))
-    outgoing = outgoing.reshape(devices, capacity, model_width)
-    received = lax.all_to_all(outgoing, "ctx", split_axis=0, concat_axis=0, tiled=True)
-    slot_count = received.shape[1]
-    rows_flat = received.reshape(devices * slot_count, model_width)
-    gate_val = jnp.dot(rows_flat, w_gate[0], preferred_element_type=jnp.float32)
-    up_val = jnp.dot(rows_flat, w_up[0], preferred_element_type=jnp.float32)
-    activated = ((up_val + 1.0) * gate_val * jax.nn.sigmoid(1.702 * gate_val)).astype(jnp.bfloat16)
-    piece = jnp.dot(activated, w_down[0], preferred_element_type=jnp.float32).astype(jnp.bfloat16)
-    returned = lax.all_to_all(
-        piece.reshape(devices, slot_count, model_width),
-        "ctx",
-        split_axis=0,
-        concat_axis=0,
-        tiled=True,
-    )
-    shard_total = (
-        returned.reshape(experts, shard_count, capacity, model_width)
-        .astype(jnp.float32)
-        .sum(axis=1)
-    )
-    summed = lax.optimization_barrier(shard_total.astype(jnp.bfloat16)).astype(jnp.float32)
-    per_choice = summed[flat_expert, slot_rank] * route_weight.reshape(-1)[:, None]
-    moe_output = (
-        features + per_choice.reshape(tok_rows, per_token, model_width).sum(axis=1)
-    ).astype(jnp.bfloat16)
+    moe_output = (features + both[:tok_rows] + both[tok_rows:]).astype(jnp.bfloat16)
     return (moe_output, attended)
 
 

time: 590 us -> 242 us (0.41)
  the two profiles are of different devices: /device:TPU:10 before, /device:TPU:0 now
where the time goes in v1:
time: 242 us; the launch traced here: 241 us
  Pallas kernels  115 us (48%)
  waiting for transfers between devices  74.3 us (31%)
  between operations  14.2 us (6%)
  matrix products  12.8 us (5%)
  starting transfers between devices  12 us (5%)
  local copies, waits for them, and re-layouts  9.6 us (4%)
  other arithmetic  3.53 us (1%)
    pallas_call x1, Pallas kernels, experts_call(): pl.pallas_call(functools.partial(expert_kernel, groups), out_shape=jax.Sh...  115 us
    all_gather x1, waiting for transfers between devices, local(): lax.all_gather(o_proj, 'ctx', axis=0, tiled=True)  72.7 us
    ppermute x3, starting transfers between devices, from_behind(): return lax.ppermute(block, axis, route)  12 us
    unnamed x13, local copies, waits for them, and re-layouts  7.8 us
    dot_general x1, matrix products, local(): jnp.dot(attended, lax.all_gather(o_proj, 'ctx', axis=0, tiled=True), pref...  6.52 us
  transfers between devices with their start and end apart: 4, of which 3 were waited for; matrix products, arithmetic and copies ran while one was open for 6% of the time, Pallas kernels for 0%

profile of v1, /device:TPU:0, one launch (start us, length us, event | category | flops | bytes accessed | tf_op | source)
XLA Modules:
  0.0 241.5 jit_solution(293084403086429073)
XLA Ops:
  7.2 0.0 copy-start
  7.2 0.0 all-gather.2.cloned.1.call-start
  7.2 0.7 all-gather.2.cloned.1.call-update
  7.9 0.8 pad_maximum_fusion
  8.7 2.3 collective-permute-start
  11.1 0.1 compare_and_fusion
  11.2 0.7 collective-permute-done
  11.9 4.9 %collective-permute-start.1 = (bf16[2,64,256]{2,1,0:T(8,128)(2,1)S(1)}, bf16[2,64,256]{2,1,0:T(8,128)(2,1)S(1)}, u32[]{:S(2)}, u32[]{:S(2)}) collective-permute-start(bf16[2,64,256]{2,1,0:T(8,128)(2,1)S(1)} %collective-permute-done), channel_id=1, source_target_pairs={{0,1},{1,2},{2,3},{3,4},{4,5},{5,6},{6,7},{7,8},{8,9},{9,10},{10,1... | collective-permute-start | bytes 196616 | tf_op jit(solution)/shard_map/ppermute | solution.py:18
  16.9 0.7 fusion.22
  17.6 0.2 collective-permute-done.1
  17.8 4.7 %collective-permute-start.2 = (bf16[2,64,256]{2,1,0:T(8,128)(2,1)S(1)}, bf16[2,64,256]{2,1,0:T(8,128)(2,1)S(1)}, u32[]{:S(2)}, u32[]{:S(2)}) collective-permute-start(bf16[2,64,256]{2,1,0:T(8,128)(2,1)S(1)} %collective-permute-done.1), channel_id=1, source_target_pairs={{0,1},{1,2},{2,3},{3,4},{4,5},{5,6},{6,7},{7,8},{8,9},{9,10},{10,1... | collective-permute-start | bytes 196616 | tf_op jit(solution)/shard_map/ppermute | solution.py:18
  22.4 0.1 convolution_convert_fusion.2
  22.6 1.5 reshape.53
  24.1 0.7 convert_element_type.56
  24.8 0.1 eq.40
  24.9 4.3 %copy.37.gate_hbm = bf16[1,2880,360]{2,1,0:T(8,128)(2,1)} copy(bf16[1,2880,360]{1,2,0:T(8,128)(2,1)} %param.16) | data formatting | bytes 4147200 | tf_op args[5]
  29.2 2.6 %copy.38.up_hbm = bf16[1,2880,360]{2,1,0:T(8,128)(2,1)} copy(bf16[1,2880,360]{1,2,0:T(8,128)(2,1)S(1)} %copy-done.1) | data formatting | bytes 4147200 | tf_op args[6]
  31.7 0.1 fusion.17
  31.9 0.1 copy.35
  32.0 0.1 copy.34
  32.1 1.0 fusion.32
  33.2 0.7 convolution_convert_fusion.1
  33.9 0.9 copy.41
  34.8 72.7 %all-gather.2.cloned.1.call-done = bf16[2048,2880]{1,0:T(8,128)(2,1)} async-done(((bf16[64,2880]{1,0:T(8,128)(2,1)}), bf16[2048,2880]{1,0:T(8,128)(2,1)}) %all-gather.2.cloned.1.call-update) | async-done | bytes 11796496 | tf_op jit(solution)/shard_map/all_gather | solution.py:306
  107.4 6.5 %multiply_reduce_fusion = (f32[64]{0:T(128)S(1)}, f32[64,2880]{1,0:T(8,128)S(1)}) fusion(bf16[64,2048]{0,1:T(8,128)(2,1)S(1)} %bitcast.59, bf16[2048,2880]{1,0:T(8,128)(2,1)} %all-gather.2.cloned.1.call-done, bf16[64,2880]{1,0:T(8,128)(2,1)S(1)} %copy-done.2), kind=kOutput, calls=%fused_computation.18 | convolution fusion | flops 756080576 | bytes 13164800 | tf_op jit(solution)/shard_map/dot_general | solution.py:304
  114.0 0.3 select_reduce_fusion
  114.3 0.1 fusion.15
  114.5 0.1 fusion.16
  114.6 2.0 convolution_convert_fusion
  116.6 115.0 %shard_map.122 = bf16[8,40,2880]{2,1,0:T(8,128)(2,1)} custom-call(bf16[8,40,2880]{2,1,0:T(8,128)(2,1)} %bitcast.56, bf16[1,2880,360]{2,1,0:T(8,128)(2,1)} %copy.37.gate_hbm, bf16[1,2880,360]{2,1,0:T(8,128)(2,1)} %copy.38.up_hbm, bf16[1,360,2880]{2,1,0:T(8,128)(2,1)} %down_hbm.1), custom_call_target="tpu_custom_call" | custom-call | tf_op jit(solution)/shard_map/pallas_call | solution.py:249
  231.6 2.2 fusion.18
  233.8 0.8 fusion.7
  (19 shorter events, 0.1 us)
Async XLA Ops:
  7.2 106.8 %copy-start = (bf16[2880,8]{0,1:T(8,128)(2,1)S(1)}, bf16[2880,8]{0,1:T(8,128)(2,1)}, u32[]{:S(2)}) copy-start(bf16[2880,8]{0,1:T(8,128)(2,1)} %param.14) | copy-start | bytes 138244
  7.2 100.3 %all-gather.2.cloned.1.call-start = ((), (), s32[]{:S(2)}) async-start(), calls=%async_computation | async-start | bytes 12435456 | tf_op jit(solution)/shard_map/all_gather | solution.py:306
  8.7 3.2 %collective-permute-start = (bf16[2,64,256]{2,1,0:T(8,128)(2,1)S(1)}, bf16[2,64,256]{2,1,0:T(8,128)(2,1)S(1)}, u32[]{:S(2)}, u32[]{:S(2)}) collective-permute-start(bf16[2,64,256]{2,1,0:T(8,128)(2,1)S(1)} %pad_maximum_fusion), channel_id=1, source_target_pairs={{0,1},{1,2},{2,3},{3,4},{4,5},{5,6},{6,7},{7,8},{8,9},{9,10},{10,1... | collective-permute-start | bytes 196616 | tf_op jit(solution)/shard_map/ppermute | solution.py:18
  11.9 5.8 %collective-permute-start.1 = (bf16[2,64,256]{2,1,0:T(8,128)(2,1)S(1)}, bf16[2,64,256]{2,1,0:T(8,128)(2,1)S(1)}, u32[]{:S(2)}, u32[]{:S(2)}) collective-permute-start(bf16[2,64,256]{2,1,0:T(8,128)(2,1)S(1)} %collective-permute-done), channel_id=1, source_target_pairs={{0,1},{1,2},{2,3},{3,4},{4,5},{5,6},{6,7},{7,8},{8,9},{9,10},{10,1... | collective-permute-start | bytes 196616 | tf_op jit(solution)/shard_map/ppermute | solution.py:18
  17.8 14.1 %collective-permute-start.2 = (bf16[2,64,256]{2,1,0:T(8,128)(2,1)S(1)}, bf16[2,64,256]{2,1,0:T(8,128)(2,1)S(1)}, u32[]{:S(2)}, u32[]{:S(2)}) collective-permute-start(bf16[2,64,256]{2,1,0:T(8,128)(2,1)S(1)} %collective-permute-done.1), channel_id=1, source_target_pairs={{0,1},{1,2},{2,3},{3,4},{4,5},{5,6},{6,7},{7,8},{8,9},{9,10},{10,1... | collective-permute-start | bytes 196616 | tf_op jit(solution)/shard_map/ppermute | solution.py:18
  24.9 4.3 %copy-start.1 = (bf16[1,2880,360]{1,2,0:T(8,128)(2,1)S(1)}, bf16[1,2880,360]{1,2,0:T(8,128)(2,1)}, u32[]{:S(2)}) copy-start(bf16[1,2880,360]{1,2,0:T(8,128)(2,1)} %param.17) | copy-start | bytes 6220804
  29.1 2.7 %copy-start.3 = (bf16[64,256]{1,0:T(8,128)(2,1)S(1)}, bf16[64,256]{1,0:T(8,128)(2,1)}, u32[]{:S(2)}) copy-start(bf16[64,256]{1,0:T(8,128)(2,1)} %param.21) | copy-start | bytes 98308
  29.2 2.7 %copy-start.4 = (bf16[64,256]{1,0:T(8,128)(2,1)S(1)}, bf16[64,256]{1,0:T(8,128)(2,1)}, u32[]{:S(2)}) copy-start(bf16[64,256]{1,0:T(8,128)(2,1)} %param.20) | copy-start | bytes 98308
  33.1 74.3 %copy-start.2 = (bf16[64,2880]{1,0:T(8,128)(2,1)S(1)}, bf16[64,2880]{1,0:T(8,128)(2,1)}, u32[]{:S(2)}) copy-start(bf16[64,2880]{1,0:T(8,128)(2,1)} %param.11) | copy-start | bytes 1105924
Sparse Core Ops, SparseCore 0:
  10.8 96.5 all-gather.1

commit v2 on v1

--- a/solution.py
+++ b/solution.py
@@ -10,33 +10,6 @@
 HEADS = 32
 KV_HEADS = 4
 HEAD_DIM = 64
-
-
-def from_behind(block, axis, distance):
-    devices = range(lax.axis_size(axis))
-    route = [(i - distance, i) for i in devices if i - distance in devices]
-    return lax.ppermute(block, axis, route)
-
-
-def attend_block(query_rows, key_rows, value_rows, span, tok_rows):
-    group_size = HEADS // KV_HEADS
-    queries = query_rows.reshape(tok_rows, KV_HEADS, group_size, HEAD_DIM)
-    key_grid = key_rows.reshape(4 * tok_rows, KV_HEADS, HEAD_DIM)
-    value_grid = value_rows.reshape(4 * tok_rows, KV_HEADS, HEAD_DIM)
-    scores = jnp.einsum(
-        "tgrd,pgd->grtp", queries, key_grid, preferred_element_type=jnp.float32
-    ) * HEAD_DIM ** (-0.5)
-    query_pos = span * tok_rows + jnp.arange(tok_rows, dtype=jnp.int32)
-    key_pos = (span - 3) * tok_rows + jnp.arange(4 * tok_rows, dtype=jnp.int32)
-    allowed = (key_pos[None, :] >= 0) & (key_pos[None, :] <= query_pos[:, None])
-    scores = jnp.where(allowed, scores, -1e30)
-    top_score = jnp.max(scores, axis=-1, keepdims=True)
-    weights = jnp.where(allowed, jnp.exp(scores - top_score), 0.0)
-    probs = (weights / jnp.sum(weights, axis=-1, keepdims=True)).astype(jnp.bfloat16)
-    mixed_heads = jnp.einsum(
-        "grtp,pgd->tgrd", probs, value_grid, preferred_element_type=jnp.float32
-    )
-    return mixed_heads.reshape(tok_rows, HEADS * HEAD_DIM).astype(jnp.bfloat16)
 
 
 MEMBERS = 4
@@ -208,8 +181,11 @@
             share_sibling(s).wait_recv()
             share_diag(s).wait_recv()
             block = recv[s].reshape(MEMBERS * rows, width)
-            gate = jnp.dot(block, gate_ref[...], preferred_element_type=jnp.float32)
-            up = jnp.dot(block, up_ref[...], preferred_element_type=jnp.float32)
+            across = (((1,), (1,)), ((), ()))
+            gate = lax.dot_general(
+                block, gate_ref[...], across, preferred_element_type=jnp.float32
+            )
+            up = lax.dot_general(block, up_ref[...], across, preferred_element_type=jnp.float32)
             activated = ((up + 1.0) * gate * jax.nn.sigmoid(1.702 * gate)).astype(jnp.bfloat16)
             for at in range(0, width, 768):
                 span = slice(at, min(at + 768, width))
@@ -239,7 +215,7 @@
 
 def experts_call(slabs, w_gate, w_up, w_down):
     groups, slots, width = slabs.shape
-    hidden = w_gate.shape[2]
+    hidden = w_gate.shape[1]
     anywhere = pl.BlockSpec(memory_space=pl.ANY)
     vmem = pl.BlockSpec(memory_space=pltpu.VMEM)
 
@@ -258,8 +234,8 @@
             buffer(groups, slots, width),
             buffer(groups, slots, width),
             buffer(groups, slots, width),
-            buffer(width, hidden),
-            buffer(width, hidden),
+            buffer(hidden, width),
+            buffer(hidden, width),
             buffer(hidden, width),
             pltpu.SemaphoreType.DMA((3,)),
             pltpu.SemaphoreType.DMA((8, groups)),
@@ -269,6 +245,266 @@
             collective_id=0, has_side_effects=True, vmem_limit_bytes=56 * 1024 * 1024
         ),
     )(slabs, w_gate, w_up, w_down)
+
+
+def attention_kernel(
+    levels,
+    wo_ref,
+    query_ref,
+    keys_ref,
+    values_ref,
+    hidden_ref,
+    gain_ref,
+    attended_ref,
+    stream_ref,
+    normed_ref,
+    wo,
+    key_window,
+    value_window,
+    mixed,
+    total,
+    kv_send,
+    kv_recv,
+    send_sem,
+    recv_sem,
+):
+    count = levels * 8
+    me = lax.axis_index("ctx")
+    level = me // 8
+    row = (me // 4) % 2
+    column = (me // 2) % 2
+    core = me % 2
+    sibling = me + 1 - 2 * core
+
+    def place(at, first, second):
+        down = first * (1 - core) + second * core
+        over = first * core + second * (1 - core)
+        return (
+            (at * 2 + row + down * (1 - 2 * row)) * 4
+            + (column + over * (1 - 2 * column)) * 2
+            + core
+        )
+
+    def send(slot, kind, index, device):
+        return pltpu.make_async_remote_copy(
+            src_ref=wo.at[slot],
+            dst_ref=wo.at[slot],
+            send_sem=send_sem.at[kind, index],
+            recv_sem=recv_sem.at[slot],
+            device_id={"ctx": device},
+            device_id_type=pl.DeviceIdType.MESH,
+        )
+
+    across, beyond = place(level, 1, 0), place(level, 0, 1)
+
+    def along(at):
+        return send(me, 0, at, place(at, 0, 0))
+
+    def to_first(at):
+        return send(place(at, 0, 0), 1, at, across)
+
+    def to_second(at, first):
+        return send(place(at, first, 0), 2 + first, at, beyond)
+
+    def to_sibling(at, first, second):
+        return send(place(at, first, second), 4 + 2 * first + second, at, sibling)
+
+    def arrived(slot):
+        send(slot, 0, 0, sibling).wait_recv()
+
+    def kv_copy(part, distance):
+        source = (keys_ref, values_ref)[part]
+        target = (key_window, value_window)[part]
+        return pltpu.make_async_remote_copy(
+            src_ref=source,
+            dst_ref=target.at[3 - distance],
+            send_sem=kv_send.at[part, distance - 1],
+            recv_sem=kv_recv.at[part, distance - 1],
+            device_id={"ctx": lax.rem(me + distance, count)},
+            device_id_type=pl.DeviceIdType.MESH,
+        )
+
+    barrier = pltpu.get_barrier_semaphore()
+
+    def greet(device):
+        pl.semaphore_signal(
+            barrier, inc=1, device_id={"ctx": device}, device_id_type=pl.DeviceIdType.MESH
+        )
+
+    @pl.loop(1, levels)
+    def _(o):
+        greet(place(lax.rem(level + o, levels), 0, 0))
+
+    for device in (sibling, across, beyond):
+        greet(device)
+    for distance in (1, 2, 3):
+        greet(lax.rem(me + distance, count))
+        greet(lax.rem(me - distance + count, count))
+    wo[me] = wo_ref[...]
+    key_window[3] = keys_ref[...]
+    value_window[3] = values_ref[...]
+    pl.semaphore_wait(barrier, levels - 1 + 9)
+
+    for distance in (1, 2, 3):
+        for part in (0, 1):
+            kv_copy(part, distance).start()
+
+    @pl.loop(1, levels)
+    def _(o):
+        along(lax.rem(level + o, levels)).start()
+
+    total[...] = jnp.zeros_like(total)
+    tok_rows = query_ref.shape[0]
+    window = 4 * tok_rows
+    width = total.shape[1]
+    block_rows = wo.shape[1]
+    group_size = HEADS // KV_HEADS
+    chunk = group_size * HEAD_DIM
+
+    def attend(g):
+        pair = pl.ds(pl.multiple_of(g // 2 * 2 * HEAD_DIM, 2 * HEAD_DIM), 2 * HEAD_DIM)
+        even = g % 2 == 0
+        key_pair = key_window[:, :, pair].reshape(window, 2 * HEAD_DIM)
+        value_pair = value_window[:, :, pair].reshape(window, 2 * HEAD_DIM)
+        head_keys = jnp.where(even, key_pair[:, :HEAD_DIM], key_pair[:, HEAD_DIM:])
+        head_values = jnp.where(even, value_pair[:, :HEAD_DIM], value_pair[:, HEAD_DIM:])
+        at = pl.ds(pl.multiple_of(g * chunk, chunk), chunk)
+        queries = query_ref[:, at]
+        query_pos = lax.broadcasted_iota(jnp.int32, (tok_rows, window), 0)
+        key_pos = lax.broadcasted_iota(jnp.int32, (tok_rows, window), 1) - 3 * tok_rows
+        allowed = (key_pos <= query_pos) & (key_pos + me * tok_rows >= 0)
+        for h in range(group_size):
+            lanes = slice(h * HEAD_DIM, (h + 1) * HEAD_DIM)
+            scores = lax.dot_general(
+                queries[:, lanes],
+                head_keys,
+                (((1,), (1,)), ((), ())),
+                preferred_element_type=jnp.float32,
+            ) * HEAD_DIM ** (-0.5)
+            scores = jnp.where(allowed, scores, -1e30)
+            top_score = jnp.max(scores, axis=-1, keepdims=True)
+            weights = jnp.where(allowed, jnp.exp(scores - top_score), 0.0)
+            probs = weights * (1.0 / jnp.sum(weights, axis=-1, keepdims=True))
+            mixed[:, lanes] = jnp.dot(
+                probs.astype(jnp.bfloat16), head_values, preferred_element_type=jnp.float32
+            ).astype(jnp.bfloat16)
+        attended_ref[:, at] = mixed[...]
+
+    def level_at(step):
+        return lax.rem(level - step + levels, levels)
+
+    @pl.loop(0, levels + 3)
+    def _(t):
+        @pl.when(t < levels)
+        def _():
+            at = level_at(t)
+
+            @pl.when(t > 0)
+            def _():
+                arrived(place(at, 0, 0))
+
+            to_first(at).start()
+            to_second(at, 0).start()
+            to_sibling(at, 0, 0).start()
+
+        @pl.when(t == 0)
+        def _():
+            for distance in (1, 2, 3):
+                for part in (0, 1):
+                    kv_copy(part, distance).wait_recv()
+
+        @pl.when((t >= 1) & (t < levels + 1))
+        def _():
+            at = level_at(t - 1)
+            arrived(place(at, 1, 0))
+            to_second(at, 1).start()
+            to_sibling(at, 1, 0).start()
+
+        @pl.when(t < KV_HEADS)
+        def _():
+            attend(t)
+
+        @pl.when((t >= 2) & (t < levels + 2))
+        def _():
+            at = level_at(t - 2)
+            for first in (0, 1):
+                arrived(place(at, first, 1))
+                to_sibling(at, first, 1).start()
+
+        @pl.when(t >= 3)
+        def _():
+            at = level_at(t - 3)
+            for group in (at * 2, at * 2 + 1):
+                for member in (0, 2):
+                    arrived(group * 4 + member + 1 - core)
+                depth = 4 * block_rows
+                rows = wo[pl.ds(group * 4, 4)].reshape(depth, width)
+                heads = attended_ref[:, pl.ds(pl.multiple_of(group * depth, depth), depth)]
+                for start in range(0, width, 768):
+                    span = slice(start, min(start + 768, width))
+                    total[:, span] += jnp.dot(
+                        heads, rows[:, span], preferred_element_type=jnp.float32
+                    )
+
+    stream = (hidden_ref[...].astype(jnp.float32) + total[...]).astype(jnp.bfloat16)
+    stream_ref[...] = stream
+    features = stream.astype(jnp.float32)
+    normed_ref[...] = (
+        features
+        * lax.rsqrt(jnp.mean(features * features, axis=-1, keepdims=True) + 1e-05)
+        * gain_ref[...].astype(jnp.float32)
+    ).astype(jnp.bfloat16)
+
+    @pl.loop(0, levels)
+    def _(at):
+        to_first(at).wait_send()
+        for first in (0, 1):
+            to_second(at, first).wait_send()
+            for second in (0, 1):
+                to_sibling(at, first, second).wait_send()
+
+    @pl.loop(1, levels)
+    def _(o):
+        along(lax.rem(level + o, levels)).wait_send()
+
+    for distance in (1, 2, 3):
+        for part in (0, 1):
+            kv_copy(part, distance).wait_send()
+
+
+def attention_call(o_proj, query, keys, values, hidden_states, norm_gain):
+    devices = lax.axis_size("ctx")
+    levels = devices // 8
+    block_rows, width = o_proj.shape
+    tok_rows = query.shape[0]
+
+    def buffer(*shape):
+        return pltpu.VMEM(shape, jnp.bfloat16)
+
+    return pl.pallas_call(
+        functools.partial(attention_kernel, levels),
+        out_shape=[
+            jax.ShapeDtypeStruct(query.shape, jnp.bfloat16),
+            jax.ShapeDtypeStruct(hidden_states.shape, jnp.bfloat16),
+            jax.ShapeDtypeStruct(hidden_states.shape, jnp.bfloat16),
+        ],
+        in_specs=[pl.BlockSpec(memory_space=pltpu.VMEM)] * 6,
+        out_specs=[pl.BlockSpec(memory_space=pltpu.VMEM)] * 3,
+        scratch_shapes=[
+            buffer(devices, block_rows, width),
+            buffer(4, tok_rows, keys.shape[1]),
+            buffer(4, tok_rows, keys.shape[1]),
+            buffer(tok_rows, HEADS // KV_HEADS * HEAD_DIM),
+            pltpu.VMEM((tok_rows, width), jnp.float32),
+            pltpu.SemaphoreType.DMA((2, 3)),
+            pltpu.SemaphoreType.DMA((2, 3)),
+            pltpu.SemaphoreType.DMA((8, levels)),
+            pltpu.SemaphoreType.DMA((devices,)),
+        ],
+        compiler_params=pltpu.CompilerParams(
+            collective_id=1, has_side_effects=True, vmem_limit_bytes=48 * 1024 * 1024
+        ),
+    )(o_proj, query, keys, values, hidden_states, norm_gain.reshape(1, -1))
 
 
 def local(
@@ -292,27 +528,10 @@
     shard_count = devices // experts
     capacity = min(tok_rows, (tok_rows * per_token // experts // shard_count + 1) * shard_count)
     slots = -(-capacity // 8) * 8
-    span = lax.axis_index("ctx")
-    kv_pair = jnp.stack([keys, values])
-    pieces = [kv_pair]
-    current = kv_pair
-    for step_index in range(3):
-        current = from_behind(current, "ctx", 1)
-        pieces.append(current)
-    window = jnp.concatenate(pieces[::-1], axis=1)
-    attended = attend_block(query, window[0], window[1], span, tok_rows)
-    projected = jnp.dot(
-        attended,
-        lax.all_gather(o_proj, "ctx", axis=0, tiled=True),
-        preferred_element_type=jnp.float32,
+    attended, stream, normed = attention_call(
+        o_proj, query, keys, values, hidden_states, norm_gain
     )
-    stream = (hidden_states.astype(jnp.float32) + projected).astype(jnp.bfloat16)
     features = stream.astype(jnp.float32)
-    normed = (
-        features
-        * lax.rsqrt(jnp.mean(features * features, axis=-1, keepdims=True) + 1e-05)
-        * norm_gain.astype(jnp.float32)
-    ).astype(jnp.bfloat16)
     logits = jnp.dot(normed, router_weight, preferred_element_type=jnp.float32)
     choices = jnp.arange(experts, dtype=jnp.int32)
     named = jnp.any(routes[:, :, None] == choices, axis=1)
@@ -328,7 +547,9 @@
     slabs = lax.dot_general(
         place, normed, (((0,), (0,)), ((), ())), preferred_element_type=jnp.float32
     ).astype(jnp.bfloat16).reshape(experts, slots, model_width)
-    summed = experts_call(slabs, w_gate, w_up, w_down).reshape(experts * slots, model_width)
+    summed = experts_call(
+        slabs, jnp.swapaxes(w_gate, 1, 2), jnp.swapaxes(w_up, 1, 2), w_down
+    ).reshape(experts * slots, model_width)
     weights = jnp.where(assign, route_weight[:, :, None], 0.0).reshape(tok_rows, experts * slots)
     upper = weights.astype(jnp.bfloat16)
     lower = (weights - upper.astype(jnp.float32)).astype(jnp.bfloat16)

time: 242 us -> 206 us (0.85)
  Pallas kernels: 115 us -> 193 us
  waiting for transfers between devices: 74.3 us -> 0 us
  between operations: 14.2 us -> 0.72 us
  starting transfers between devices: 12 us -> 0 us
  matrix products: 12.8 us -> 4.43 us
  local copies, waits for them, and re-layouts: 9.6 us -> 5.95 us
    all_gather x1 -> x0, waiting for transfers between devices: 72.7 us -> none  [local(): lax.all_gather(o_proj, 'ctx', axis=0, tiled=True)]
    pallas_call x0 -> x1, Pallas kernels: none -> 64.1 us  [attention_call(): pl.pallas_call(functools.partial(attention_kernel, levels), out_shape=[ja...]
    pallas_call x1, Pallas kernels: 115 us -> 128 us  [experts_call(): pl.pallas_call(functools.partial(expert_kernel, groups), out_shape=jax.Sh...]
    ppermute x3 -> x0, starting transfers between devices: 12 us -> none  [from_behind(): return lax.ppermute(block, axis, route)]
    dot_general x2 -> x0, matrix products: 7.22 us -> none  [the longest x1 6.52 us: local(): jnp.dot(attended, lax.all_gather(o_proj, 'ctx', axis=0, tiled=True), pref...]
    unnamed x13, local copies, waits for them, and re-layouts: 7.8 us -> 5.15 us
  transfers between devices with their start and end apart: 4 -> 0, of which waited for: 3 -> 0; matrix products, arithmetic and copies ran while one was open for 6% -> 0% of each run, Pallas kernels for 0% -> 0%
where the time goes in v2:
time: 206 us
  Pallas kernels  193 us (94%)
  local copies, waits for them, and re-layouts  5.95 us (3%)
  matrix products  4.43 us (2%)
    pallas_call x1, Pallas kernels, experts_call(): pl.pallas_call(functools.partial(expert_kernel, groups), out_shape=jax.Sh...  128 us
    pallas_call x1, Pallas kernels, attention_call(): pl.pallas_call(functools.partial(attention_kernel, levels), out_shape=[ja...  64.1 us
    unnamed x13, local copies, waits for them, and re-layouts  5.15 us

profile of v2, /device:TPU:0, one launch (start us, length us, event | category | flops | bytes accessed | tf_op | source)
XLA Modules:
  0.0 205.6 jit_solution(6669654078040327983)
XLA Ops:
  0.6 0.0 copy-start
  0.6 0.7 fusion.9
  1.3 0.1 convolution_convert_fusion.1
  1.5 0.1 eq.40
  1.6 0.7 reshape.28.gain_ref
  2.3 0.1 fusion.4
  2.4 0.0 copy-start.1
  2.4 1.0 copy-done.1
  3.4 0.0 copy-start.2
  3.4 1.0 copy-done.2
  4.4 0.0 copy-start.3
  4.4 0.9 copy-done.3
  5.3 0.0 copy-start.4
  5.3 0.8 copy-done.4
  6.1 0.0 copy-start.5
  6.1 0.8 copy-done.5
  6.8 64.1 %shard_map.122 = (bf16[64,2048]{1,0:T(8,128)(2,1)S(1)}, bf16[64,2880]{1,0:T(8,128)(2,1)S(1)}, bf16[64,2880]{1,0:T(8,128)(2,1)S(1)}) custom-call(bf16[64,2880]{1,0:T(8,128)(2,1)S(1)} %copy-done.1, bf16[64,2048]{1,0:T(8,128)(2,1)S(1)} %copy-done.3, bf16[64,256]{1,0:T(8,128)(2,1)S(1)} %copy-done.4, bf16[64,256]{1,0:T(8,128)(2,1)S(1)} %copy-done.5, ...), custom_call_target="tpu_custom_call" | custom-call | tf_op jit(solution)/shard_map/pallas_call | solution.py:484
  71.0 0.0 copy-done
  71.0 0.2 select_reduce_fusion
  71.3 0.1 fusion.3
  71.4 0.1 fusion.2
  71.5 1.9 convolution_convert_fusion
  73.4 128.5 %shard_map.123 = bf16[8,40,2880]{2,1,0:T(8,128)(2,1)} custom-call(bf16[8,40,2880]{2,1,0:T(8,128)(2,1)} %bitcast.35, bf16[1,360,2880]{2,1,0:T(8,128)(2,1)} %bitcast.36, bf16[1,360,2880]{2,1,0:T(8,128)(2,1)} %bitcast.37, bf16[1,360,2880]{2,1,0:T(8,128)(2,1)} %down_hbm.1), custom_call_target="tpu_custom_call" | custom-call | tf_op jit(solution)/shard_map/pallas_call | solution.py:225
  201.9 2.2 %fusion.5 = f32[128,2880]{1,0:T(8,128)S(1)} fusion(bf16[320,2880]{1,0:T(8,128)(2,1)} %bitcast.34, bf16[64,320]{0,1:T(8,128)(2,1)S(1)} %fusion.3, bf16[64,320]{0,1:T(8,128)(2,1)S(1)} %fusion.2), kind=kOutput, calls=%fused_computation.11 | convolution fusion | flops 236093440 | bytes 3399680 | tf_op jit(solution)/shard_map/dot_general | solution.py:556
  204.1 0.8 fusion
  204.9 0.7 copy.28
  (3 shorter events, 0.1 us)
Async XLA Ops:
  0.6 70.3 %copy-start = (bf16[2880,8]{0,1:T(8,128)(2,1)S(1)}, bf16[2880,8]{0,1:T(8,128)(2,1)}, u32[]{:S(2)}) copy-start(bf16[2880,8]{0,1:T(8,128)(2,1)} %param.14) | copy-start | bytes 138244
  2.4 1.0 copy-start.1
  3.4 1.0 copy-start.2
  4.4 0.9 copy-start.3
  5.3 0.8 copy-start.4
  6.1 0.8 copy-start.5

commit v3 on v2

--- a/solution.py
+++ b/solution.py
@@ -13,6 +13,16 @@
 
 
 MEMBERS = 4
+AHEAD_GATHER = 2
+AHEAD_EXPERTS = 2
+
+
+def xor(a, b, count):
+    result, bit = 0, 1
+    while bit < count:
+        result += (a // bit + b // bit) % 2 * bit
+        bit *= 2
+    return result
 
 
 def expert_kernel(
@@ -110,14 +120,14 @@
     def given_back(s):
         return to(final.at[s], out_ref.at[s], 7, s, s, s * MEMBERS + j)
 
-    @pl.loop(1, groups)
+    def source(step):
+        return xor(group, step, groups)
+
+    @pl.loop(1, min(AHEAD_EXPERTS + 1, groups))
     def _(o):
-        scatter(lax.rem(group + o, groups)).start()
+        scatter(source(o)).start()
 
     recv[group, j] = slab_ref[group]
-
-    def source(step):
-        return lax.rem(group - step + groups, groups)
 
     rows, width = recv.shape[2], recv.shape[3]
 
@@ -132,6 +142,11 @@
                 scattered(s).wait_recv()
 
             share_partner(s).start()
+
+            @pl.when((t > 0) & (t + AHEAD_EXPERTS < groups))
+            def _():
+                scatter(source(t + AHEAD_EXPERTS)).start()
+
             share_sibling(s).start()
 
         @pl.when((t >= 1) & (t < groups + 1))
@@ -249,12 +264,12 @@
 
 def attention_kernel(
     levels,
-    wo_ref,
-    query_ref,
-    keys_ref,
-    values_ref,
-    hidden_ref,
-    gain_ref,
+    wo_hbm,
+    query_hbm,
+    keys_hbm,
+    values_hbm,
+    hidden_hbm,
+    gain_hbm,
     attended_ref,
     stream_ref,
     normed_ref,
@@ -263,6 +278,10 @@
     value_window,
     mixed,
     total,
+    query_ref,
+    hidden_ref,
+    gain_ref,
+    load_sem,
     kv_send,
     kv_recv,
     send_sem,
@@ -295,7 +314,25 @@
             device_id_type=pl.DeviceIdType.MESH,
         )
 
+    loads = [
+        pltpu.make_async_copy(src, dst, load_sem.at[i])
+        for i, (src, dst) in enumerate(
+            (
+                (wo_hbm, wo.at[me]),
+                (keys_hbm, key_window.at[3]),
+                (values_hbm, value_window.at[3]),
+                (query_hbm, query_ref),
+                (hidden_hbm, hidden_ref),
+                (gain_hbm, gain_ref),
+            )
+        )
+    ]
+    for load in loads:
+        load.start()
     across, beyond = place(level, 1, 0), place(level, 0, 1)
+
+    def level_at(step):
+        return xor(level, step, levels)
 
     def along(at):
         return send(me, 0, at, place(at, 0, 0))
@@ -313,10 +350,9 @@
         send(slot, 0, 0, sibling).wait_recv()
 
     def kv_copy(part, distance):
-        source = (keys_ref, values_ref)[part]
         target = (key_window, value_window)[part]
         return pltpu.make_async_remote_copy(
-            src_ref=source,
+            src_ref=target.at[3],
             dst_ref=target.at[3 - distance],
             send_sem=kv_send.at[part, distance - 1],
             recv_sem=kv_recv.at[part, distance - 1],
@@ -340,20 +376,21 @@
     for distance in (1, 2, 3):
         greet(lax.rem(me + distance, count))
         greet(lax.rem(me - distance + count, count))
-    wo[me] = wo_ref[...]
-    key_window[3] = keys_ref[...]
-    value_window[3] = values_ref[...]
+    for load in loads[:3]:
+        load.wait()
     pl.semaphore_wait(barrier, levels - 1 + 9)
 
     for distance in (1, 2, 3):
         for part in (0, 1):
             kv_copy(part, distance).start()
 
-    @pl.loop(1, levels)
+    @pl.loop(1, min(AHEAD_GATHER + 1, levels))
     def _(o):
-        along(lax.rem(level + o, levels)).start()
+        along(level_at(o)).start()
 
     total[...] = jnp.zeros_like(total)
+    for load in loads[3:]:
+        load.wait()
     tok_rows = query_ref.shape[0]
     window = 4 * tok_rows
     width = total.shape[1]
@@ -390,9 +427,6 @@
             ).astype(jnp.bfloat16)
         attended_ref[:, at] = mixed[...]
 
-    def level_at(step):
-        return lax.rem(level - step + levels, levels)
-
     @pl.loop(0, levels + 3)
     def _(t):
         @pl.when(t < levels)
@@ -405,6 +439,11 @@
 
             to_first(at).start()
             to_second(at, 0).start()
+
+            @pl.when((t > 0) & (t + AHEAD_GATHER < levels))
+            def _():
+                along(level_at(t + AHEAD_GATHER)).start()
+
             to_sibling(at, 0, 0).start()
 
         @pl.when(t == 0)
@@ -488,7 +527,7 @@
             jax.ShapeDtypeStruct(hidden_states.shape, jnp.bfloat16),
             jax.ShapeDtypeStruct(hidden_states.shape, jnp.bfloat16),
         ],
-        in_specs=[pl.BlockSpec(memory_space=pltpu.VMEM)] * 6,
+        in_specs=[pl.BlockSpec(memory_space=pl.ANY)] * 6,
         out_specs=[pl.BlockSpec(memory_space=pltpu.VMEM)] * 3,
         scratch_shapes=[
             buffer(devices, block_rows, width),
@@ -496,13 +535,17 @@
             buffer(4, tok_rows, keys.shape[1]),
             buffer(tok_rows, HEADS // KV_HEADS * HEAD_DIM),
             pltpu.VMEM((tok_rows, width), jnp.float32),
+            buffer(*query.shape),
+            buffer(*hidden_states.shape),
+            buffer(1, width),
+            pltpu.SemaphoreType.DMA((6,)),
             pltpu.SemaphoreType.DMA((2, 3)),
             pltpu.SemaphoreType.DMA((2, 3)),
             pltpu.SemaphoreType.DMA((8, levels)),
             pltpu.SemaphoreType.DMA((devices,)),
         ],
         compiler_params=pltpu.CompilerParams(
-            collective_id=1, has_side_effects=True, vmem_limit_bytes=48 * 1024 * 1024
+            collective_id=1, has_side_effects=True, vmem_limit_bytes=56 * 1024 * 1024
         ),
     )(o_proj, query, keys, values, hidden_states, norm_gain.reshape(1, -1))
 

time: 206 us -> 200 us (0.971)
  the two profiles are of different devices: /device:TPU:0 before, /device:TPU:10 now
where the time goes in v3:
time: 200 us; the launch traced here: 199 us
  Pallas kernels  188 us (94%)
  matrix products  6.45 us (3%)
  local copies, waits for them, and re-layouts  2.22 us (1%)
    pallas_call x1, Pallas kernels, experts_call(): pl.pallas_call(functools.partial(expert_kernel, groups), out_shape=jax.Sh...  126 us
    pallas_call x1, Pallas kernels, attention_call(): pl.pallas_call(functools.partial(attention_kernel, levels), out_shape=[ja...  62.2 us

profile of v3, /device:TPU:10, one launch (start us, length us, event | category | flops | bytes accessed | tf_op | source)
XLA Modules:
  0.0 199.3 jit_solution(424295526283411210)
XLA Ops:
  0.6 0.0 copy-start
  0.6 0.7 fusion.9
  1.3 0.1 convolution_convert_fusion.1
  1.5 0.1 eq.40
  1.6 1.3 reshape.28.gain_hbm
  2.9 0.1 fusion.4
  3.0 62.2 %shard_map.122 = (bf16[64,2048]{1,0:T(8,128)(2,1)}, bf16[64,2880]{1,0:T(8,128)(2,1)}, bf16[64,2880]{1,0:T(8,128)(2,1)}) custom-call(bf16[64,2880]{1,0:T(8,128)(2,1)} %wo_hbm.1, bf16[64,2048]{1,0:T(8,128)(2,1)} %query_hbm.1, bf16[64,256]{1,0:T(8,128)(2,1)} %keys_hbm.1, bf16[64,256]{1,0:T(8,128)(2,1)} %values_hbm.1, bf16[64,2880]{1,0:T(8,128)(2,1)} %hidden_hbm.1, ...), custom_call_target="tpu_custom_call" | custom-call | tf_op jit(solution)/shard_map/pallas_call | solution.py:523
  65.2 0.0 copy-done
  65.2 1.2 select_reduce_fusion
  66.5 0.1 fusion.3
  66.6 0.1 fusion.2
  66.7 2.9 %convolution_convert_fusion = bf16[320,2880]{1,0:T(8,128)(2,1)} fusion(pred[64,320]{0,1:T(32,128)(4,1)S(1)} %fusion.4, bf16[64,2880]{1,0:T(8,128)(2,1)} %get-tuple-element.6), kind=kOutput, calls=%fused_computation | convolution fusion | flops 118886400 | bytes 2232320 | tf_op jit(solution)/shard_map/dot_general | solution.py:590
  69.6 125.8 %shard_map.123 = bf16[8,40,2880]{2,1,0:T(8,128)(2,1)} custom-call(bf16[8,40,2880]{2,1,0:T(8,128)(2,1)} %bitcast.35, bf16[1,360,2880]{2,1,0:T(8,128)(2,1)} %bitcast.36, bf16[1,360,2880]{2,1,0:T(8,128)(2,1)} %bitcast.37, bf16[1,360,2880]{2,1,0:T(8,128)(2,1)} %down_hbm.1), custom_call_target="tpu_custom_call" | custom-call | tf_op jit(solution)/shard_map/pallas_call | solution.py:240
  195.4 0.0 copy-start.1
  195.4 2.2 %fusion.5 = f32[128,2880]{1,0:T(8,128)S(1)} fusion(bf16[320,2880]{1,0:T(8,128)(2,1)} %bitcast.34, bf16[64,320]{0,1:T(8,128)(2,1)S(1)} %fusion.3, bf16[64,320]{0,1:T(8,128)(2,1)S(1)} %fusion.2), kind=kOutput, calls=%fused_computation.11 | convolution fusion | flops 236093440 | bytes 3399680 | tf_op jit(solution)/shard_map/dot_general | solution.py:599
  197.6 0.0 copy-done.1
  197.7 0.0 copy-start.2
  197.7 0.8 fusion
  198.5 0.1 copy-done.2
  198.6 0.7 copy.28
  (3 shorter events, 0.1 us)
Async XLA Ops:
  0.6 64.6 %copy-start = (bf16[2880,8]{0,1:T(8,128)(2,1)S(1)}, bf16[2880,8]{0,1:T(8,128)(2,1)}, u32[]{:S(2)}) copy-start(bf16[2880,8]{0,1:T(8,128)(2,1)} %param.14) | copy-start | bytes 138244
  195.4 2.3 %copy-start.1 = (bf16[64,2880]{1,0:T(8,128)(2,1)S(1)}, bf16[64,2880]{1,0:T(8,128)(2,1)}, u32[]{:S(2)}) copy-start(bf16[64,2880]{1,0:T(8,128)(2,1)} %get-tuple-element.5) | copy-start | bytes 1105924
  197.7 1.0 copy-start.2

commit v4 on v3

--- a/solution.py
+++ b/solution.py
@@ -27,7 +27,8 @@
 
 def expert_kernel(
     groups,
-    slab_ref,
+    normed_ref,
+    place_ref,
     gate_hbm,
     up_hbm,
     down_hbm,
@@ -41,6 +42,9 @@
     gate_ref,
     up_ref,
     down_ref,
+    dense,
+    placed,
+    cross,
     weight_sem,
     send_sem,
     recv_sem,
@@ -88,13 +92,36 @@
     greet(partner)
     pl.semaphore_wait(barrier, groups + 1)
 
-    def scatter(target):
+    levels = groups // 2
+    level, row = group // 2, group % 2
+
+    def whole(kind, src, dst, at, there):
+        return to(src, dst, kind, at, there, (at * 2 + row) * MEMBERS + j)
+
+    def send_block(at):
+        return (
+            whole(0, normed_ref, dense.at[level], at, level),
+            whole(8, place_ref.at[pl.ds(at * 2, 2)], placed.at[level], at, level),
+        )
+
+    def block_arrived(at):
+        return (
+            whole(0, normed_ref, dense.at[at], at, at),
+            whole(8, place_ref.at[pl.ds(at * 2, 2)], placed.at[at], at, at),
+        )
+
+    def send_cross(at):
         return to(
-            slab_ref.at[target], recv.at[group, j], 0, target, group, target * MEMBERS + j
-        )
-
-    def scattered(s):
-        return to(slab_ref.at[s], recv.at[s, j], 0, s, s, sibling)
+            cross.at[at],
+            recv.at[at * 2 + row, j],
+            9,
+            at,
+            at,
+            (level * 2 + 1 - row) * MEMBERS + j,
+        )
+
+    def level_at(step):
+        return xor(level, step, levels)
 
     def share_sibling(s):
         return to(recv.at[s, j], recv.at[s, j], 1, s, s, sibling)
@@ -123,11 +150,13 @@
     def source(step):
         return xor(group, step, groups)
 
-    @pl.loop(1, min(AHEAD_EXPERTS + 1, groups))
+    @pl.loop(1, min(AHEAD_EXPERTS + 1, levels))
     def _(o):
-        scatter(source(o)).start()
-
-    recv[group, j] = slab_ref[group]
+        for copy in send_block(level_at(o)):
+            copy.start()
+
+    dense[level] = normed_ref[...]
+    placed[level] = place_ref[pl.ds(level * 2, 2)]
 
     rows, width = recv.shape[2], recv.shape[3]
 
@@ -137,16 +166,33 @@
         def _():
             s = source(t)
 
-            @pl.when(t > 0)
+            at = s // 2
+
+            @pl.when(t % 2 == 0)
             def _():
-                scattered(s).wait_recv()
+                @pl.when(t > 0)
+                def _():
+                    for copy in block_arrived(at):
+                        copy.wait_recv()
+
+                @pl.when((t > 0) & (t // 2 + AHEAD_EXPERTS < levels))
+                def _():
+                    for copy in send_block(level_at(t // 2 + AHEAD_EXPERTS)):
+                        copy.start()
+
+                cross[at] = jnp.dot(
+                    placed[at, 1 - row], dense[at], preferred_element_type=jnp.float32
+                ).astype(jnp.bfloat16)
+                send_cross(at).start()
+                recv[s, j] = jnp.dot(
+                    placed[at, row], dense[at], preferred_element_type=jnp.float32
+                ).astype(jnp.bfloat16)
+
+            @pl.when(t % 2 == 1)
+            def _():
+                send_cross(at).wait_recv()
 
             share_partner(s).start()
-
-            @pl.when((t > 0) & (t + AHEAD_EXPERTS < groups))
-            def _():
-                scatter(source(t + AHEAD_EXPERTS)).start()
-
             share_sibling(s).start()
 
         @pl.when((t >= 1) & (t < groups + 1))
@@ -220,16 +266,25 @@
         piece_diag(s).wait_send()
         piece_far(s).wait_send()
 
+    @pl.loop(0, levels)
+    def _(at):
+        send_cross(at).wait_send()
+
+    @pl.loop(1, levels)
+    def _(o):
+        for copy in send_block(level_at(o)):
+            copy.wait_send()
+
     @pl.loop(1, groups)
     def _(o):
         s = source(o)
-        scattered(s).wait_send()
         given_back(s).wait_send()
         given_back(s).wait_recv()
 
 
-def experts_call(slabs, w_gate, w_up, w_down):
-    groups, slots, width = slabs.shape
+def experts_call(normed, place, w_gate, w_up, w_down):
+    groups, slots, tok_rows = place.shape
+    width = normed.shape[1]
     hidden = w_gate.shape[1]
     anywhere = pl.BlockSpec(memory_space=pl.ANY)
     vmem = pl.BlockSpec(memory_space=pltpu.VMEM)
@@ -239,8 +294,8 @@
 
     return pl.pallas_call(
         functools.partial(expert_kernel, groups),
-        out_shape=jax.ShapeDtypeStruct(slabs.shape, jnp.bfloat16),
-        in_specs=[vmem, anywhere, anywhere, anywhere],
+        out_shape=jax.ShapeDtypeStruct((groups, slots, width), jnp.bfloat16),
+        in_specs=[vmem, vmem, anywhere, anywhere, anywhere],
         out_specs=vmem,
         scratch_shapes=[
             buffer(groups, MEMBERS, slots, width),
@@ -252,14 +307,17 @@
             buffer(hidden, width),
             buffer(hidden, width),
             buffer(hidden, width),
+            buffer(groups // 2, tok_rows, width),
+            buffer(groups // 2, 2, slots, tok_rows),
+            buffer(groups // 2, slots, width),
             pltpu.SemaphoreType.DMA((3,)),
-            pltpu.SemaphoreType.DMA((8, groups)),
-            pltpu.SemaphoreType.DMA((8, groups)),
+            pltpu.SemaphoreType.DMA((10, groups)),
+            pltpu.SemaphoreType.DMA((10, groups)),
         ],
         compiler_params=pltpu.CompilerParams(
             collective_id=0, has_side_effects=True, vmem_limit_bytes=56 * 1024 * 1024
         ),
-    )(slabs, w_gate, w_up, w_down)
+    )(normed, place, w_gate, w_up, w_down)
 
 
 def attention_kernel(
@@ -586,12 +644,9 @@
     rank = jnp.dot(earlier, named.astype(jnp.bfloat16), preferred_element_type=jnp.float32)
     slot_index = jnp.arange(slots, dtype=jnp.int32)
     assign = named[:, :, None] & (rank.astype(jnp.int32)[:, :, None] == slot_index)
-    place = assign.astype(jnp.bfloat16).reshape(tok_rows, experts * slots)
-    slabs = lax.dot_general(
-        place, normed, (((0,), (0,)), ((), ())), preferred_element_type=jnp.float32
-    ).astype(jnp.bfloat16).reshape(experts, slots, model_width)
+    place = jnp.transpose(assign.astype(jnp.bfloat16), (1, 2, 0))
     summed = experts_call(
-        slabs, jnp.swapaxes(w_gate, 1, 2), jnp.swapaxes(w_up, 1, 2), w_down
+        normed, place, jnp.swapaxes(w_gate, 1, 2), jnp.swapaxes(w_up, 1, 2), w_down
     ).reshape(experts * slots, model_width)
     weights = jnp.where(assign, route_weight[:, :, None], 0.0).reshape(tok_rows, experts * slots)
     upper = weights.astype(jnp.bfloat16)

time: 200 us -> 197 us (0.985)
  matrix products: 6.45 us -> 3.56 us
    dot_general x1 -> x0, matrix products: 2.89 us -> none  [local(): lax.dot_general(place, normed, (((0,), (0,)), ((), ())), preferred_elemen...]
where the time goes in v4:
time: 197 us
  Pallas kernels  188 us (95%)
  matrix products  3.56 us (2%)
  other arithmetic  2.49 us (1%)
  local copies, waits for them, and re-layouts  2.22 us (1%)
    pallas_call x1, Pallas kernels, experts_call(): pl.pallas_call(functools.partial(expert_kernel, groups), out_shape=jax.Sh...  126 us
    pallas_call x1, Pallas kernels, attention_call(): pl.pallas_call(functools.partial(attention_kernel, levels), out_shape=[ja...  62.2 us

profile of v4, /device:TPU:10, one launch (start us, length us, event | category | flops | bytes accessed | tf_op | source)
XLA Modules:
  0.0 196.8 jit_solution(10658895296444266014)
XLA Ops:
  0.6 0.0 copy-start
  0.6 0.7 fusion.11
  1.3 0.1 convolution_convert_fusion
  1.5 0.1 eq.46
  1.6 1.3 reshape.21.gain_hbm
  2.9 0.7 fusion.5.place_ref
  3.5 62.2 %shard_map.122 = (bf16[64,2048]{1,0:T(8,128)(2,1)}, bf16[64,2880]{1,0:T(8,128)(2,1)}, bf16[64,2880]{1,0:T(8,128)(2,1)}) custom-call(bf16[64,2880]{1,0:T(8,128)(2,1)} %wo_hbm.1, bf16[64,2048]{1,0:T(8,128)(2,1)} %query_hbm.1, bf16[64,256]{1,0:T(8,128)(2,1)} %keys_hbm.1, bf16[64,256]{1,0:T(8,128)(2,1)} %values_hbm.1, bf16[64,2880]{1,0:T(8,128)(2,1)} %hidden_hbm.1, ...), custom_call_target="tpu_custom_call" | custom-call | tf_op jit(solution)/shard_map/pallas_call | solution.py:581
  65.8 0.0 copy-done
  65.8 1.2 select_reduce_fusion
  67.0 0.1 fusion.3
  67.2 0.1 fusion.2
  67.3 125.6 %shard_map.123 = bf16[8,40,2880]{2,1,0:T(8,128)(2,1)} custom-call(bf16[64,2880]{1,0:T(8,128)(2,1)} %get-tuple-element.6.normed_ref, bf16[8,40,64]{2,1,0:T(8,128)(2,1)} %fusion.5.place_ref, bf16[1,360,2880]{2,1,0:T(8,128)(2,1)} %bitcast.38, bf16[1,360,2880]{2,1,0:T(8,128)(2,1)} %bitcast.39, bf16[1,360,2880]{2,1,0:T(8,128)(2,1)} %down_hbm.1), custom_call_target="tpu_custom_call" | custom-call | tf_op jit(solution)/shard_map/pallas_call | solution.py:295
  192.9 0.0 copy-start.1
  192.9 2.2 %fusion.7 = f32[128,2880]{1,0:T(8,128)S(1)} fusion(bf16[320,2880]{1,0:T(8,128)(2,1)} %bitcast.37, bf16[64,320]{0,1:T(8,128)(2,1)S(1)} %fusion.3, bf16[64,320]{0,1:T(8,128)(2,1)S(1)} %fusion.2), kind=kOutput, calls=%fused_computation.13 | convolution fusion | flops 236093440 | bytes 3399680 | tf_op jit(solution)/shard_map/dot_general | solution.py:654
  195.2 0.0 copy-done.1
  195.2 0.0 copy-start.2
  195.2 0.8 fusion
  196.0 0.1 copy-done.2
  196.1 0.7 copy.26
  (3 shorter events, 0.1 us)
Async XLA Ops:
  0.6 65.1 %copy-start = (bf16[2880,8]{0,1:T(8,128)(2,1)S(1)}, bf16[2880,8]{0,1:T(8,128)(2,1)}, u32[]{:S(2)}) copy-start(bf16[2880,8]{0,1:T(8,128)(2,1)} %param.14) | copy-start | bytes 138244
  192.9 2.3 %copy-start.1 = (bf16[64,2880]{1,0:T(8,128)(2,1)S(1)}, bf16[64,2880]{1,0:T(8,128)(2,1)}, u32[]{:S(2)}) copy-start(bf16[64,2880]{1,0:T(8,128)(2,1)} %get-tuple-element.5) | copy-start | bytes 1105924
  195.2 1.0 copy-start.2

commit v5 on v4

--- a/solution.py
+++ b/solution.py
@@ -162,6 +162,35 @@
 
     @pl.loop(0, groups + 4)
     def _(t):
+        @pl.when((t >= 4) & (t < groups + 4))
+        def _():
+            s = source(t - 4)
+            piece_far(s).wait_recv()
+            total = (
+                pieces[s, j].astype(jnp.float32)
+                + near[s, 0].astype(jnp.float32)
+                + far[s].astype(jnp.float32)
+            ).astype(jnp.bfloat16)
+
+            @pl.when(t == 4)
+            def _():
+                out_ref[group] = total
+
+            @pl.when(t > 4)
+            def _():
+                final[s] = total
+                give_back(s).start()
+
+        @pl.when((t >= 3) & (t < groups + 3))
+        def _():
+            s = source(t - 3)
+            piece_near(s).wait_recv()
+            piece_diag(s).wait_recv()
+            pair_sum[s] = (
+                pieces[s, j_far].astype(jnp.float32) + near[s, 1].astype(jnp.float32)
+            ).astype(jnp.bfloat16)
+            piece_far(s).start()
+
         @pl.when(t < groups)
         def _():
             s = source(t)
@@ -200,35 +229,6 @@
             s = source(t - 1)
             share_partner(s).wait_recv()
             share_diag(s).start()
-
-        @pl.when((t >= 4) & (t < groups + 4))
-        def _():
-            s = source(t - 4)
-            piece_far(s).wait_recv()
-            total = (
-                pieces[s, j].astype(jnp.float32)
-                + near[s, 0].astype(jnp.float32)
-                + far[s].astype(jnp.float32)
-            ).astype(jnp.bfloat16)
-
-            @pl.when(t == 4)
-            def _():
-                out_ref[group] = total
-
-            @pl.when(t > 4)
-            def _():
-                final[s] = total
-                give_back(s).start()
-
-        @pl.when((t >= 3) & (t < groups + 3))
-        def _():
-            s = source(t - 3)
-            piece_near(s).wait_recv()
-            piece_diag(s).wait_recv()
-            pair_sum[s] = (
-                pieces[s, j_far].astype(jnp.float32) + near[s, 1].astype(jnp.float32)
-            ).astype(jnp.bfloat16)
-            piece_far(s).start()
 
         @pl.when((t >= 2) & (t < groups + 2))
         def _():

time: 197 us -> 195 us (0.990)
  Pallas kernels: 188 us -> 185 us
    pallas_call x1, Pallas kernels: 126 us -> 123 us  [experts_call(): pl.pallas_call(functools.partial(expert_kernel, groups), out_shape=jax.Sh...]
where the time goes in v5:
time: 195 us; the launch traced here: 194 us
  Pallas kernels  185 us (95%)
  matrix products  3.56 us (2%)
  other arithmetic  2.49 us (1%)
  local copies, waits for them, and re-layouts  2.22 us (1%)
    pallas_call x1, Pallas kernels, experts_call(): pl.pallas_call(functools.partial(expert_kernel, groups), out_shape=jax.Sh...  123 us
    pallas_call x1, Pallas kernels, attention_call(): pl.pallas_call(functools.partial(attention_kernel, levels), out_shape=[ja...  62.2 us

profile of v5, /device:TPU:10, one launch (start us, length us, event | category | flops | bytes accessed | tf_op | source)
XLA Modules:
  0.0 194.0 jit_solution(15960787246927623740)
XLA Ops:
  0.6 0.0 copy-start
  0.6 0.7 fusion.11
  1.3 0.1 convolution_convert_fusion
  1.5 0.1 eq.46
  1.6 1.3 reshape.21.gain_hbm
  2.9 0.7 fusion.5.place_ref
  3.5 62.2 %shard_map.122 = (bf16[64,2048]{1,0:T(8,128)(2,1)}, bf16[64,2880]{1,0:T(8,128)(2,1)}, bf16[64,2880]{1,0:T(8,128)(2,1)}) custom-call(bf16[64,2880]{1,0:T(8,128)(2,1)} %wo_hbm.1, bf16[64,2048]{1,0:T(8,128)(2,1)} %query_hbm.1, bf16[64,256]{1,0:T(8,128)(2,1)} %keys_hbm.1, bf16[64,256]{1,0:T(8,128)(2,1)} %values_hbm.1, bf16[64,2880]{1,0:T(8,128)(2,1)} %hidden_hbm.1, ...), custom_call_target="tpu_custom_call" | custom-call | tf_op jit(solution)/shard_map/pallas_call | solution.py:581
  65.8 0.0 copy-done
  65.8 1.2 select_reduce_fusion
  67.0 0.1 fusion.3
  67.2 0.1 fusion.2
  67.3 122.8 %shard_map.123 = bf16[8,40,2880]{2,1,0:T(8,128)(2,1)} custom-call(bf16[64,2880]{1,0:T(8,128)(2,1)} %get-tuple-element.6.normed_ref, bf16[8,40,64]{2,1,0:T(8,128)(2,1)} %fusion.5.place_ref, bf16[1,360,2880]{2,1,0:T(8,128)(2,1)} %bitcast.38, bf16[1,360,2880]{2,1,0:T(8,128)(2,1)} %bitcast.39, bf16[1,360,2880]{2,1,0:T(8,128)(2,1)} %down_hbm.1), custom_call_target="tpu_custom_call" | custom-call | tf_op jit(solution)/shard_map/pallas_call | solution.py:295
  190.1 0.0 copy-start.1
  190.1 2.2 %fusion.7 = f32[128,2880]{1,0:T(8,128)S(1)} fusion(bf16[320,2880]{1,0:T(8,128)(2,1)} %bitcast.37, bf16[64,320]{0,1:T(8,128)(2,1)S(1)} %fusion.3, bf16[64,320]{0,1:T(8,128)(2,1)S(1)} %fusion.2), kind=kOutput, calls=%fused_computation.13 | convolution fusion | flops 236093440 | bytes 3399680 | tf_op jit(solution)/shard_map/dot_general | solution.py:654
  192.3 0.0 copy-done.1
  192.3 0.0 copy-start.2
  192.4 0.8 fusion
  193.2 0.1 copy-done.2
  193.3 0.7 copy.26
  (3 shorter events, 0.1 us)
Async XLA Ops:
  0.6 65.1 %copy-start = (bf16[2880,8]{0,1:T(8,128)(2,1)S(1)}, bf16[2880,8]{0,1:T(8,128)(2,1)}, u32[]{:S(2)}) copy-start(bf16[2880,8]{0,1:T(8,128)(2,1)} %param.14) | copy-start | bytes 138244
  190.1 2.3 %copy-start.1 = (bf16[64,2880]{1,0:T(8,128)(2,1)S(1)}, bf16[64,2880]{1,0:T(8,128)(2,1)}, u32[]{:S(2)}) copy-start(bf16[64,2880]{1,0:T(8,128)(2,1)} %get-tuple-element.5) | copy-start | bytes 1105924
  192.3 1.0 copy-start.2
